TPU v7x, 512 devices: a whole 4x4x16 slice. The times are simulated.
512 devices in a mesh: row: 32 (over x, z_lo, core), col: 16 (over z_hi, y).
Axes of the slice: x: 4, y: 4, z: 16 (z_hi: 4, z_lo: 4; z = z_hi * 4 + z_lo), core: 2. Of those that a mesh axis runs over, the one named last changes fastest.
Arguments:
- solution: float32 [8, 2048, 2048], P(None, 'row', 'col'), may hold values from -1 to 1, as said below
- search: float32 [8, 2048, 2048], P(None, 'row', 'col'), may hold values from -1 to 1, as said below
- basis: float32 [8, 2048, 2048], P(None, 'row', 'col'), may hold values from -1 to 1, as said below
- resid_a: float32 [2048, 2048], P('row', 'col'), may hold values from -1 to 1, as said below
- resid_b: float32 [2048, 2048], P('row', 'col'), may hold values from -1 to 1, as said below
- scalars: float32 [3], replicated, may hold values from 0.5 to 2
- profile_a: float32 [8, 512], replicated, may hold values from -0.25 to 0.25
- profile_b: float32 [8, 512], replicated, may hold values from -0.25 to 0.25
- source_mask: int32 [2048, 2048], P('row', 'col'), may hold values 0 or 1
- weight_code: int32 [2048, 2048], P('row', 'col'), may hold values from 0 to 7
- roll_code: int32 [2048, 2048], P('row', 'col'), may hold values from 0 to 2
Outputs:
- next_solution: float32 [8, 2048, 2048], P(None, 'row', 'col')
- next_search: float32 [8, 2048, 2048], P(None, 'row', 'col')
- next_basis: float32 [8, 2048, 2048], P(None, 'row', 'col')
- next_resid_a: float32 [2048, 2048], P('row', 'col')
- next_resid_b: float32 [2048, 2048], P('row', 'col')
Inputs may be any that keep to these rules, and one draw needn't show every extreme that they name: `solution`: the whole array has Euclidean norm 1. `search`: the whole array has Euclidean norm 1. `basis`: the whole array has Euclidean norm 1. Euclidean norm sqrt(1/2), so that resid_a and resid_b together have norm 1. Euclidean norm sqrt(1/2), so that resid_a and resid_b together have norm 1.
All inputs are finite; a program needn't handle non-finite values. No bound on the sum of `source_mask` on one device may be relied on, other than what follows from the above.
Results may differ from a plain program's by a relative error of at most 0.000078.
Values sent between devices are 32-bit elements; how exact they have to be, the bound alone decides.
A program may use at most 64 MiB of HBM per device.

v0:
```python
import functools

import jax
import jax.numpy as jnp
from jax import lax
from jax.experimental import pallas as pl
from jax.experimental.pallas import tpu as pltpu
from jax.sharding import Mesh
from jax.sharding import PartitionSpec as P

X, Z, C, H, Y = "row_0", "row_1", "row_2", "col_0", "col_1"
ROW = (X, Z, C)
COL = (H, Y)
MESH = pl.DeviceIdType.MESH
f32 = jnp.float32
bf16 = jnp.bfloat16
EPS = 1e-12

K, L, R, W = 8, 512, 64, 128
CL = 5
EXT = CL * W

NEAR = [(dz, dc) for dz in range(4) for dc in range(2)][1:]
PLANE = [(dx, dy) for dx in range(4) for dy in range(4)][1:]
FAR = [1, 2, 3]


def split(x):
    hi = x.astype(bf16)
    return hi, (x - hi.astype(f32)).astype(bf16)


def dot(a, b, ca, cb):
    return lax.dot_general(a, b, (((ca,), (cb,)), ((), ())), preferred_element_type=f32)


def kernel(
    basis, resid_a, resid_b, scal, pa, pb, mask, wcode, rcode,
    raw_v, raw_a, raw_b, coef,
    src_r, src_c, ta_hi, ta_lo, tb_hi, tb_lo, wext_a, wext_b,
    even, odd, r1, r2, r3, cp, c1, c2, ext_c, ext_e, ext_o,
    own, g_near, g_plane, g_far, send_sem, recv_sem,
):
    x, z, c, h, y = (lax.axis_index(a) for a in (X, Z, C, H, Y))
    started = []

    def near(o):
        return {Z: lax.rem(z + o[0], 4), C: lax.rem(c + o[1], 2)}

    def plane(o):
        return {X: lax.rem(x + o[0], 4), Y: lax.rem(y + o[1], 4)}

    def far(o):
        return {H: lax.rem(h + o, 4)}

    def copy(src, dst, to, again=False):
        i = len(started) - again
        d = pltpu.make_async_remote_copy(
            src_ref=src, dst_ref=dst, send_sem=send_sem.at[i], recv_sem=recv_sem.at[i], device_id=to, device_id_type=MESH
        )
        if not again:
            started.append(d)
        return d

    barrier = pltpu.get_barrier_semaphore()
    peers = [near(o) for o in NEAR] + [plane(o) for o in PLANE] + [far(o) for o in FAR]
    for to in peers:
        pl.semaphore_signal(barrier, inc=1, device_id=to, device_id_type=MESH)

    m = mask[...].astype(f32)
    pad = jnp.zeros((1, EXT - L), f32)
    for k in range(K):
        hi, lo = split(basis[k] * m)
        src_r[0:R, k * W : (k + 1) * W] = hi
        src_r[R : 2 * R, k * W : (k + 1) * W] = lo
        src_c[k * R : (k + 1) * R, 0:W] = hi
        src_c[k * R : (k + 1) * R, W : 2 * W] = lo
        row = jnp.concatenate([pb[k : k + 1, :], pad], axis=1)
        t = pltpu.roll(jnp.broadcast_to(row, (R, EXT)), 0, 1, stride=1, stride_axis=0)
        hi, lo = split(t)
        tb_hi[k * R : (k + 1) * R, :] = hi
        tb_lo[k * R : (k + 1) * R, :] = lo
    part = dot(tb_hi[...], src_c[...], 0, 0) + dot(tb_lo[...], src_c[...], 0, 0)
    part = part[:, :W] + part[:, W:]
    for level in range(9):
        block = part[level * R : (level + 1) * R]
        if level % 2:
            odd[level // 2] = block
        else:
            even[level // 2] = block

    pl.semaphore_wait(barrier, len(peers))
    to_core = near((0, 1))
    s_r1 = copy(odd, r1, to_core)
    s_r1.start()

    for k in range(K):
        row = jnp.concatenate([pa[k : k + 1, :], pad], axis=1)
        t = pltpu.roll(jnp.broadcast_to(row, (W, EXT)), 0, 1, stride=1, stride_axis=0)
        hi, lo = split(t)
        ta_hi[k * W : (k + 1) * W, :] = hi
        ta_lo[k * W : (k + 1) * W, :] = lo
    part = dot(src_r[...], ta_hi[...], 1, 0) + dot(src_r[...], ta_lo[...], 1, 0)
    part = part[:R] + part[R:]
    for level in range(CL):
        cp[level] = part[:, level * W : (level + 1) * W]
    s_c1 = [copy(cp.at[d], c1.at[d], plane((0, d))) for d in (1, 2, 3)]
    for s in s_c1:
        s.start()

    s_r1.wait_recv()
    for i in range(4):
        even[1 - c + i] = even[1 - c + i] + r1[i]
    s_r2 = [copy(even.at[d], r2.at[d], near((d, 0))) for d in (1, 2, 3)]
    for s in s_r2:
        s.start()

    for s in s_c1:
        s.wait_recv()
    here, there = cp[0], cp[4]
    for d in (1, 2, 3):
        mine = d <= y
        here = here + jnp.where(mine, c1[d], 0.0)
        there = there + jnp.where(mine, 0.0, c1[d])
    cp[4] = there
    s_c2 = copy(cp.at[4], c2, far(1))
    s_c2.start()

    for s in s_r2:
        s.wait_recv()
    rows_here, there = even[0], even[4]
    for d in (1, 2, 3):
        mine = d <= z
        rows_here = rows_here + jnp.where(mine, r2[d], 0.0)
        there = there + jnp.where(mine, 0.0, r2[d])
    even[4] = there
    s_r3 = copy(even.at[4], r3, plane((1, 0)))
    s_r3.start()

    alpha = scal[0]
    base = 1.0 / (1.0 + 0.25 * wcode[...].astype(f32))
    weight_a = jnp.where(rcode[...] != 2, base, 0.0)
    weight_b = jnp.where(rcode[...] != 1, base, 0.0)

    s_c2.wait_recv()
    image = here + jnp.where(h > 0, c2[...], 0.0)
    ra = weight_a * image - alpha * resid_a[...]
    raw_a[...] = ra
    wa = weight_a * ra
    ext_c[0] = wa
    s_d1 = copy(ext_c.at[0], ext_c.at[4], far(3))
    s_d1.start()
    s_d2 = []
    for d in (1, 2, 3):
        to = plane((0, d))
        s = copy(ext_c.at[0], ext_c.at[4 - d], to)
        later = copy(ext_c.at[4], ext_c.at[4 - d], to, again=True)
        s_d2.append((s, later, y + d >= 4))
    for s, later, now in s_d2:
        pl.when(now)(s.start)

    s_r3.wait_recv()
    image = rows_here + jnp.where(x > 0, r3[...], 0.0)
    rb = weight_b * image - alpha * resid_b[...]
    raw_b[...] = rb
    wb = weight_b * rb
    ext_e[0] = wb
    s_a1 = copy(ext_e.at[0], ext_e.at[4], plane((3, 0)))
    s_a1.start()
    s_a2 = []
    for d in (1, 2, 3):
        to = near((d, 0))
        s = copy(ext_e.at[0], ext_e.at[4 - d], to)
        later = copy(ext_e.at[4], ext_e.at[4 - d], to, again=True)
        s_a2.append((s, later, z + d >= 4))
    for s, later, now in s_a2:
        pl.when(now)(s.start)

    def begin(n, tile):
        own[n, 0] = tile
        out = [copy(own.at[n, 0], g_near.at[n, i], near(o)) for i, o in enumerate(NEAR)]
        for s in out:
            s.start()
        return out

    def middle(n, out):
        for s in out:
            s.wait_recv()
        tile = own[n, 0]
        for i in range(len(NEAR)):
            tile = tile + g_near[n, i]
        own[n, 1] = tile
        out = [copy(own.at[n, 1], g_plane.at[n, i], plane(o)) for i, o in enumerate(PLANE)]
        for s in out:
            s.start()
        return out

    def last(n, out):
        for s in out:
            s.wait_recv()
        tile = own[n, 1]
        for i in range(len(PLANE)):
            tile = tile + g_plane[n, i]
        own[n, 2] = tile
        out = [copy(own.at[n, 2], g_far.at[n, i], far(o)) for i, o in enumerate(FAR)]
        for s in out:
            s.start()
        return out

    def total(n, out):
        for s in out:
            s.wait_recv()
        tile = own[n, 2]
        for i in range(len(FAR)):
            tile = tile + g_far[n, i]
        return jnp.sum(jnp.sum(tile, axis=1, keepdims=True), axis=0, keepdims=True)

    sq = ra * ra + rb * rb
    out = begin(0, jnp.sum(sq.reshape(R // 8, 8, W), axis=0))

    s_d1.wait_recv()
    ext_c[4] = jnp.where(h < 3, ext_c[4], 0.0)
    for s, later, now in s_d2:
        pl.when(jnp.logical_not(now))(later.start)
    s_a1.wait_recv()
    ext_e[4] = jnp.where(x < 3, ext_e[4], 0.0)
    for s, later, now in s_a2:
        pl.when(jnp.logical_not(now))(later.start)

    def put_a(level, block):
        hi, lo = split(block)
        wext_a[0:R, level * W : (level + 1) * W] = hi
        wext_a[R : 2 * R, level * W : (level + 1) * W] = lo

    def put_b(level, block):
        hi, lo = split(block)
        wext_b[level * R : (level + 1) * R, 0:W] = hi
        wext_b[level * R : (level + 1) * R, W : 2 * W] = lo

    put_a(0, wa)
    put_a(4, ext_c[4])
    put_b(0, wb)
    put_b(8, ext_e[4])
    put_b(9, jnp.zeros((R, W), f32))
    out = middle(0, out)

    for s, _, _ in s_a2:
        s.wait_recv()
    s_a3 = copy(ext_e.at[pl.ds(1 - c, 4)], ext_o, to_core)
    s_a3.start()
    for d in (1, 2, 3):
        put_b(2 * d, ext_e[d])
    for s, _, _ in s_d2:
        s.wait_recv()
    for d in (1, 2, 3):
        put_a(d, ext_c[d])
    ga = dot(wext_a[...], ta_hi[...], 1, 1) + dot(wext_a[...], ta_lo[...], 1, 1)
    ga = ga[:R] + ga[R:]
    for k in range(K):
        raw_v[k] = ga[:, k * W : (k + 1) * W]
    out = last(0, out)
    s_a3.wait_recv()
    for d in range(4):
        put_b(2 * d + 1, ext_o[d])
    gb = dot(tb_hi[...], wext_b[...], 1, 0) + dot(tb_lo[...], wext_b[...], 1, 0)
    gb = gb[:, :W] + gb[:, W:]
    beta = jnp.sqrt(total(0, out) + EPS)
    inv_beta = 1.0 / beta
    scaled = m * inv_beta
    sq = jnp.zeros((R, W), f32)
    for k in range(K):
        v = scaled * (raw_v[k] + gb[k * R : (k + 1) * R]) - beta * basis[k]
        raw_v[k] = v
        sq = sq + v * v
    out = begin(1, jnp.sum(sq.reshape(R // 8, 8, W), axis=0))
    out = middle(1, out)
    out = last(1, out)
    alpha_next = jnp.sqrt(total(1, out) + EPS)
    phibar, rhobar = scal[1], scal[2]
    rho = jnp.sqrt(rhobar * rhobar + beta * beta)
    cosine = rhobar / rho
    sine = beta / rho
    theta = sine * alpha_next
    phi = cosine * phibar
    for i, value in enumerate((inv_beta, 1.0 / alpha_next, phi / rho, theta / rho)):
        coef[i : i + 1, :] = jnp.broadcast_to(value, (1, W))
    coef[4:8, :] = jnp.zeros((4, W), f32)
    for s in started:
        s.wait_send()


N_COPIES = 18 + 2 * (len(NEAR) + len(PLANE) + len(FAR))


def finish(raw_v, raw_a, raw_b, coef, sol, search, sol_o, search_o, basis_o, resid_a, resid_b):
    inv_beta, inv_alpha = coef[0:1, :], coef[1:2, :]
    step, turn = coef[2:3, :], coef[3:4, :]
    w = search[...]
    v = raw_v[...] * inv_alpha
    sol_o[...] = sol[...] + step * w
    basis_o[...] = v
    search_o[...] = v - turn * w
    resid_a[...] = raw_a[...] * inv_beta
    resid_b[...] = raw_b[...] * inv_beta


def body(sol, search, basis, resid_a, resid_b, scal, pa, pb, mask, wcode, rcode):
    vmem = pl.BlockSpec(memory_space=pltpu.VMEM)
    smem = pl.BlockSpec(memory_space=pltpu.SMEM)
    image = jax.ShapeDtypeStruct((R, W), f32)
    maps = jax.ShapeDtypeStruct((K, R, W), f32)
    raw_v, raw_a, raw_b, coef = pl.pallas_call(
        kernel,
        out_shape=(maps, image, image, jax.ShapeDtypeStruct((8, W), f32)),
        in_specs=[vmem, vmem, vmem, smem, vmem, vmem, vmem, vmem, vmem],
        out_specs=(vmem, vmem, vmem, vmem),
        scratch_shapes=[
            pltpu.VMEM((2 * R, K * W), bf16),
            pltpu.VMEM((K * R, 2 * W), bf16),
            pltpu.VMEM((K * W, EXT), bf16),
            pltpu.VMEM((K * W, EXT), bf16),
            pltpu.VMEM((K * R, EXT), bf16),
            pltpu.VMEM((K * R, EXT), bf16),
            pltpu.VMEM((2 * R, EXT), bf16),
            pltpu.VMEM((EXT, 2 * W), bf16),
            pltpu.VMEM((5, R, W), f32),
            pltpu.VMEM((4, R, W), f32),
            pltpu.VMEM((4, R, W), f32),
            pltpu.VMEM((4, R, W), f32),
            pltpu.VMEM((R, W), f32),
            pltpu.VMEM((5, R, W), f32),
            pltpu.VMEM((4, R, W), f32),
            pltpu.VMEM((R, W), f32),
            pltpu.VMEM((5, R, W), f32),
            pltpu.VMEM((5, R, W), f32),
            pltpu.VMEM((4, R, W), f32),
            pltpu.VMEM((2, 3, 8, W), f32),
            pltpu.VMEM((2, len(NEAR), 8, W), f32),
            pltpu.VMEM((2, len(PLANE), 8, W), f32),
            pltpu.VMEM((2, len(FAR), 8, W), f32),
            pltpu.SemaphoreType.DMA((N_COPIES,)),
            pltpu.SemaphoreType.DMA((N_COPIES,)),
        ],
        compiler_params=pltpu.CompilerParams(
            collective_id=0, has_side_effects=True, vmem_limit_bytes=48 * 1024 * 1024
        ),
    )(basis, resid_a, resid_b, scal, pa, pb, mask, wcode, rcode)
    return pl.pallas_call(
        finish,
        out_shape=(maps, maps, maps, image, image),
        in_specs=[vmem] * 6,
        out_specs=(vmem,) * 5,
        compiler_params=pltpu.CompilerParams(vmem_limit_bytes=16 * 1024 * 1024),
    )(raw_v, raw_a, raw_b, coef, sol, search)


def solution(mesh):
    torus = Mesh(mesh.devices.reshape(4, 4, 2, 4, 4), (X, Z, C, H, Y))
    maps, image = P(None, ROW, COL), P(ROW, COL)
    return jax.shard_map(
        body,
        mesh=torus,
        in_specs=(maps, maps, maps, image, image, P(), P(), P(), image, image, image),
        out_specs=(maps, maps, maps, image, image),
        check_vma=False,
    )
```

profile of v0, /device:TPU:1, one launch (start us, length us, event | category | flops | bytes accessed | tf_op | source)
XLA Modules:
  0.0 73.0 jit_solution(448214017334496143)
XLA Ops:
  0.6 0.0 copy-start
  0.6 0.9 %copy-done = f32[8,64,128]{2,1,0:T(8,128)S(1)} copy-done((f32[8,64,128]{2,1,0:T(8,128)S(1)}, f32[8,64,128]{2,1,0:T(8,128)}, u32[]{:S(2)}) %copy-start) | copy-done | bytes 262168
  1.6 0.0 copy-start.3
  1.6 0.8 %copy-done.3 = f32[64,128]{1,0:T(8,128)S(1)} copy-done((f32[64,128]{1,0:T(8,128)S(1)}, f32[64,128]{1,0:T(8,128)}, u32[]{:S(2)}) %copy-start.3) | copy-done | bytes 32792
  2.3 0.0 copy-start.4
  2.3 0.8 %copy-done.4 = f32[64,128]{1,0:T(8,128)S(1)} copy-done((f32[64,128]{1,0:T(8,128)S(1)}, f32[64,128]{1,0:T(8,128)}, u32[]{:S(2)}) %copy-start.4) | copy-done | bytes 32792
  3.1 0.0 copy-start.5
  3.1 0.8 %copy-done.5 = s32[64,128]{1,0:T(8,128)S(1)} copy-done((s32[64,128]{1,0:T(8,128)S(1)}, s32[64,128]{1,0:T(8,128)}, u32[]{:S(2)}) %copy-start.5) | copy-done | bytes 32792
  3.9 0.0 copy-start.6
  3.9 0.8 %copy-done.6 = s32[64,128]{1,0:T(8,128)S(1)} copy-done((s32[64,128]{1,0:T(8,128)S(1)}, s32[64,128]{1,0:T(8,128)}, u32[]{:S(2)}) %copy-start.6) | copy-done | bytes 32792
  4.6 0.0 copy-start.7
  4.6 0.8 %copy-done.7 = s32[64,128]{1,0:T(8,128)S(1)} copy-done((s32[64,128]{1,0:T(8,128)S(1)}, s32[64,128]{1,0:T(8,128)}, u32[]{:S(2)}) %copy-start.7) | copy-done | bytes 32792
  5.4 0.0 copy-start.8
  5.4 0.7 copy-done.8
  6.1 0.0 copy-start.9
  6.1 0.7 copy-done.9
  6.8 0.0 copy-start.10
  6.8 0.7 copy-done.10
  7.5 0.0 copy-start.1
  7.5 63.6 %shard_map.146 = (f32[8,64,128]{2,1,0:T(8,128)S(1)}, f32[64,128]{1,0:T(8,128)S(1)}, f32[64,128]{1,0:T(8,128)S(1)}, f32[8,128]{1,0:T(8,128)S(1)}) custom-call(f32[8,64,128]{2,1,0:T(8,128)S(1)} %copy-done, f32[64,128]{1,0:T(8,128)S(1)} %copy-done.3, f32[64,128]{1,0:T(8,128)S(1)} %copy-done.4, f32[3]{0:T(128)S(1)} %copy-done.10, f32[8,512]{1,0:T(8,128)S(1)} %copy-done.8, ...), custom_call_target="tpu_custom_call" | custom-call | tf_op jit(solution)/shard_map/pallas_call | solution.py:312
  71.1 0.0 copy-done.1
  71.1 0.0 copy-start.2
  71.1 0.9 %copy-done.2 = f32[8,64,128]{2,1,0:T(8,128)S(1)} copy-done((f32[8,64,128]{2,1,0:T(8,128)S(1)}, f32[8,64,128]{2,1,0:T(8,128)}, u32[]{:S(2)}) %copy-start.2) | copy-done | bytes 262168
  72.0 0.9 %shard_map.147 = (f32[8,64,128]{2,1,0:T(8,128)}, f32[8,64,128]{2,1,0:T(8,128)}, f32[8,64,128]{2,1,0:T(8,128)}, f32[64,128]{1,0:T(8,128)}, f32[64,128]{1,0:T(8,128)}) custom-call(f32[8,64,128]{2,1,0:T(8,128)S(1)} %get-tuple-element.9.raw_v, f32[64,128]{1,0:T(8,128)S(1)} %get-tuple-element.10.raw_a, f32[64,128]{1,0:T(8,128)S(1)} %get-tuple-element.11.raw_b, ...), custom_call_target="tpu_custom_call" | custom-call | tf_op jit(solution)/shard_map/pallas_call | solution.py:348
Async XLA Ops:
  0.6 1.0 %copy-start = (f32[8,64,128]{2,1,0:T(8,128)S(1)}, f32[8,64,128]{2,1,0:T(8,128)}, u32[]{:S(2)}) copy-start(f32[8,64,128]{2,1,0:T(8,128)} %basis.1) | copy-start | bytes 786436
  1.6 0.8 %copy-start.3 = (f32[64,128]{1,0:T(8,128)S(1)}, f32[64,128]{1,0:T(8,128)}, u32[]{:S(2)}) copy-start(f32[64,128]{1,0:T(8,128)} %resid_a.1) | copy-start | bytes 98308
  2.3 0.8 %copy-start.4 = (f32[64,128]{1,0:T(8,128)S(1)}, f32[64,128]{1,0:T(8,128)}, u32[]{:S(2)}) copy-start(f32[64,128]{1,0:T(8,128)} %resid_b.1) | copy-start | bytes 98308
  3.1 0.8 %copy-start.5 = (s32[64,128]{1,0:T(8,128)S(1)}, s32[64,128]{1,0:T(8,128)}, u32[]{:S(2)}) copy-start(s32[64,128]{1,0:T(8,128)} %mask.1) | copy-start | bytes 98308
  3.9 0.8 %copy-start.6 = (s32[64,128]{1,0:T(8,128)S(1)}, s32[64,128]{1,0:T(8,128)}, u32[]{:S(2)}) copy-start(s32[64,128]{1,0:T(8,128)} %wcode.1) | copy-start | bytes 98308
  4.6 0.8 %copy-start.7 = (s32[64,128]{1,0:T(8,128)S(1)}, s32[64,128]{1,0:T(8,128)}, u32[]{:S(2)}) copy-start(s32[64,128]{1,0:T(8,128)} %rcode.1) | copy-start | bytes 98308
  5.4 0.7 copy-start.8
  6.1 0.7 copy-start.9
  6.8 0.7 copy-start.10
  7.5 63.6 %copy-start.1 = (f32[8,64,128]{2,1,0:T(8,128)S(1)}, f32[8,64,128]{2,1,0:T(8,128)}, u32[]{:S(2)}) copy-start(f32[8,64,128]{2,1,0:T(8,128)} %sol.1) | copy-start | bytes 786436
  71.1 1.0 %copy-start.2 = (f32[8,64,128]{2,1,0:T(8,128)S(1)}, f32[8,64,128]{2,1,0:T(8,128)}, u32[]{:S(2)}) copy-start(f32[8,64,128]{2,1,0:T(8,128)} %search.1) | copy-start | bytes 786436
where the time goes:
time: 73.6 us; the launch traced here: 73 us
  Pallas kernels  64.5 us (88%)
  local copies, waits for them, and re-layouts  7.77 us (11%)
    pallas_call x1, Pallas kernels, body(): pl.pallas_call(kernel, out_shape=(maps, image, image, jax.ShapeDtypeStruc...  63.6 us
    unnamed x22, local copies, waits for them, and re-layouts  7.77 us

commit v1 on v0

v1 whole, which is shorter than its diff:
```python
import jax
import jax.numpy as jnp
from jax import lax
from jax.experimental import pallas as pl
from jax.experimental.pallas import tpu as pltpu
from jax.sharding import Mesh
from jax.sharding import PartitionSpec as P

X, Z, C, H, Y = "row_0", "row_1", "row_2", "col_0", "col_1"
ROW = (X, Z, C)
COL = (H, Y)
MESH = pl.DeviceIdType.MESH
f32 = jnp.float32
bf16 = jnp.bfloat16
EPS = 1e-12

K, L, R, W = 8, 512, 64, 128
CL = 5
EXT = CL * W


def ring(a, n):
    return min(a, n - a)


PLANE = [(dx, dy, dc) for dx in range(4) for dy in range(4) for dc in range(2)][1:]
PLANE.sort(key=lambda o: -(ring(o[0], 4) + ring(o[1], 4)))
LINE = sorted(range(1, 16), key=lambda d: -ring(d, 16))


def split(x):
    hi = x.astype(bf16)
    return hi, (x - hi.astype(f32)).astype(bf16)


def dot(a, b, ca, cb):
    return lax.dot_general(a, b, (((ca,), (cb,)), ((), ())), preferred_element_type=f32)


def kernel(
    basis_h, resid_a_h, resid_b_h, scal_h, pa_h, pb_h, mask_h, wcode_h, rcode_h,
    raw_v_h, raw_a_h, raw_b_h, coef_h,
    raw_v, raw_a, raw_b, coef, basis, resid_a, resid_b, scal, pa, pb, mask, wcode, rcode,
    src_r, src_c, ta_hi, ta_lo, tb_hi, tb_lo, wext_a, wext_b,
    even, odd, r1, r2, r3, cp, c1, c2, ext_c, ext_e, ext_o,
    sums_plane, sums_line, send_sem, recv_sem, load_sem,
):
    x, z, c, h, y = (lax.axis_index(a) for a in (X, Z, C, H, Y))
    started = []

    def core():
        return {C: 1 - c}

    def run(d):
        return {Z: lax.rem(z + d, 4)}

    def along_x(d):
        return {X: lax.rem(x + d, 4)}

    def along_y(d):
        return {Y: lax.rem(y + d, 4)}

    def far(d):
        return {H: lax.rem(h + d, 4)}

    def plane(o):
        return {X: lax.rem(x + o[0], 4), Y: lax.rem(y + o[1], 4), C: lax.rem(c + o[2], 2)}

    def line(d):
        at = 4 * h + z + d
        return {H: lax.rem(at // 4, 4), Z: lax.rem(at, 4)}

    def copy(src, dst, to, again=False):
        i = len(started) - again
        d = pltpu.make_async_remote_copy(
            src_ref=src, dst_ref=dst, send_sem=send_sem.at[i], recv_sem=recv_sem.at[i], device_id=to, device_id_type=MESH
        )
        if not again:
            started.append(d)
        return d

    barrier = pltpu.get_barrier_semaphore()
    peers = [core()] + [run(d) for d in (1, 2, 3)] + [along_y(d) for d in (1, 2, 3)]
    peers += [along_x(1), along_x(3), far(1), far(3)]
    for to in peers:
        pl.semaphore_signal(barrier, inc=1, device_id=to, device_id_type=MESH)

    pairs = (
        (pa_h, pa), (pb_h, pb), (mask_h, mask), (basis_h, basis), (scal_h, scal), (wcode_h, wcode),
        (rcode_h, rcode), (resid_a_h, resid_a), (resid_b_h, resid_b),
    )
    loads = [pltpu.make_async_copy(a, b, load_sem.at[i]) for i, (a, b) in enumerate(pairs)]
    for s in loads:
        s.start()

    pad = jnp.zeros((1, EXT - L), f32)

    def table(profile, k, rows):
        row = jnp.concatenate([profile[k : k + 1, :], pad], axis=1)
        return split(pltpu.roll(jnp.broadcast_to(row, (rows, EXT)), 0, 1, stride=1, stride_axis=0))

    loads[0].wait()
    for k in range(K):
        ta_hi[k * W : (k + 1) * W, :], ta_lo[k * W : (k + 1) * W, :] = table(pa, k, W)
    loads[1].wait()
    for k in range(K):
        tb_hi[k * R : (k + 1) * R, :], tb_lo[k * R : (k + 1) * R, :] = table(pb, k, R)

    loads[2].wait()
    loads[3].wait()
    m = mask[...].astype(f32)
    for k in range(K):
        hi, lo = split(basis[k] * m)
        src_r[0:R, k * W : (k + 1) * W] = hi
        src_r[R : 2 * R, k * W : (k + 1) * W] = lo
        src_c[k * R : (k + 1) * R, 0:W] = hi
        src_c[k * R : (k + 1) * R, W : 2 * W] = lo

    part = dot(src_r[...], ta_hi[...], 1, 0) + dot(src_r[...], ta_lo[...], 1, 0)
    part = part[:R] + part[R:]
    for level in range(CL):
        cp[level] = part[:, level * W : (level + 1) * W]
    pl.semaphore_wait(barrier, len(peers))
    s_c1 = [copy(cp.at[d], c1.at[d], along_y(d)) for d in (2, 1, 3)]
    for s in s_c1:
        s.start()

    part = dot(tb_hi[...], src_c[...], 0, 0) + dot(tb_lo[...], src_c[...], 0, 0)
    part = part[:, :W] + part[:, W:]
    for level in range(9):
        block = part[level * R : (level + 1) * R]
        if level % 2:
            odd[level // 2] = block
        else:
            even[level // 2] = block
    s_r1 = copy(odd, r1, core())
    s_r1.start()
    for s in loads[4:]:
        s.wait()
    alpha = scal[0]
    base = 1.0 / (1.0 + 0.25 * wcode[...].astype(f32))
    weight_a = jnp.where(rcode[...] != 2, base, 0.0)
    weight_b = jnp.where(rcode[...] != 1, base, 0.0)

    s_r1.wait_recv()
    for i in range(4):
        even[1 - c + i] = even[1 - c + i] + r1[i]
    s_r2 = [copy(even.at[d], r2.at[d], run(d)) for d in (1, 2, 3)]
    for s in s_r2:
        s.start()

    for s in s_c1:
        s.wait_recv()
    here, there = cp[0], cp[4]
    for d in (1, 2, 3):
        mine = d <= y
        here = here + jnp.where(mine, c1[d], 0.0)
        there = there + jnp.where(mine, 0.0, c1[d])
    cp[4] = there
    s_c2 = copy(cp.at[4], c2, far(1))
    s_c2.start()

    for s in s_r2:
        s.wait_recv()
    rows_here, there = even[0], even[4]
    for d in (1, 2, 3):
        mine = d <= z
        rows_here = rows_here + jnp.where(mine, r2[d], 0.0)
        there = there + jnp.where(mine, 0.0, r2[d])
    even[4] = there
    s_r3 = copy(even.at[4], r3, along_x(1))
    s_r3.start()

    s_c2.wait_recv()
    image = here + jnp.where(h > 0, c2[...], 0.0)
    ra = weight_a * image - alpha * resid_a[...]
    raw_a[...] = ra
    wa = weight_a * ra
    ext_c[0] = wa
    s_d1 = copy(ext_c.at[0], ext_c.at[4], far(3))
    s_d1.start()
    s_d2 = []
    for d in (1, 2, 3):
        to = along_y(d)
        s = copy(ext_c.at[0], ext_c.at[4 - d], to)
        later = copy(ext_c.at[4], ext_c.at[4 - d], to, again=True)
        s_d2.append((s, later, y + d >= 4))
    for s, later, now in s_d2:
        pl.when(now)(s.start)

    s_r3.wait_recv()
    image = rows_here + jnp.where(x > 0, r3[...], 0.0)
    rb = weight_b * image - alpha * resid_b[...]
    raw_b[...] = rb
    wb = weight_b * rb
    ext_e[0] = wb
    s_a1 = copy(ext_e.at[0], ext_e.at[4], along_x(3))
    s_a1.start()
    s_a2 = []
    for d in (1, 2, 3):
        to = run(d)
        s = copy(ext_e.at[0], ext_e.at[4 - d], to)
        later = copy(ext_e.at[4], ext_e.at[4 - d], to, again=True)
        s_a2.append((s, later, z + d >= 4))
    for s, later, now in s_a2:
        pl.when(now)(s.start)

    def tile_of(q):
        t = jnp.sum(q.reshape(-1, 8, W), axis=0)
        t = t + pltpu.roll(t, 64, 1)
        return t + pltpu.roll(t, 32, 1)

    rr = tile_of(ra * ra + rb * rb)
    sq = jnp.zeros((R, W), f32)
    for k in range(K):
        sq = sq + basis[k] * basis[k]
    vv = tile_of(sq)

    s_d1.wait_recv()
    ext_c[4] = jnp.where(h < 3, ext_c[4], 0.0)
    for s, later, now in s_d2:
        pl.when(jnp.logical_not(now))(later.start)
    s_a1.wait_recv()
    ext_e[4] = jnp.where(x < 3, ext_e[4], 0.0)
    for s, later, now in s_a2:
        pl.when(jnp.logical_not(now))(later.start)

    def put_a(level, block):
        hi, lo = split(block)
        wext_a[0:R, level * W : (level + 1) * W] = hi
        wext_a[R : 2 * R, level * W : (level + 1) * W] = lo

    def put_b(level, block):
        hi, lo = split(block)
        wext_b[level * R : (level + 1) * R, 0:W] = hi
        wext_b[level * R : (level + 1) * R, W : 2 * W] = lo

    put_a(0, wa)
    put_a(4, ext_c[4])
    put_b(0, wb)
    put_b(8, ext_e[4])
    put_b(9, jnp.zeros((R, W), f32))

    for s, _, _ in s_a2:
        s.wait_recv()
    s_a3 = copy(ext_e.at[pl.ds(1 - c, 4)], ext_o, core())
    s_a3.start()
    for d in (1, 2, 3):
        put_b(2 * d, ext_e[d])
    for s, _, _ in s_d2:
        s.wait_recv()
    for d in (1, 2, 3):
        put_a(d, ext_c[d])
    ga = dot(wext_a[...], ta_hi[...], 1, 1) + dot(wext_a[...], ta_lo[...], 1, 1)
    ga = ga[:R] + ga[R:]
    for k in range(K):
        raw_v[k] = ga[:, k * W : (k + 1) * W]
    s_a3.wait_recv()
    for d in range(4):
        put_b(2 * d + 1, ext_o[d])
    gb = dot(tb_hi[...], wext_b[...], 1, 0) + dot(tb_lo[...], wext_b[...], 1, 0)
    gb = gb[:, :W] + gb[:, W:]
    zz = jnp.zeros((R, W), f32)
    zv = jnp.zeros((R, W), f32)
    for k in range(K):
        g = m * (raw_v[k] + gb[k * R : (k + 1) * R])
        raw_v[k] = g
        zz = zz + g * g
        zv = zv + g * basis[k]

    stores = [(raw_v, raw_v_h), (raw_a, raw_a_h), (raw_b, raw_b_h), (coef, coef_h)]
    stores = [pltpu.make_async_copy(a, b, load_sem.at[i]) for i, (a, b) in enumerate(stores)]

    quarter = lax.broadcasted_iota(jnp.int32, (8, W), 1) // (W // 4)
    both = jnp.where(quarter == 0, rr, vv)
    tile = jnp.where(quarter == 2, tile_of(zz), jnp.where(quarter == 3, tile_of(zv), both))
    sums_plane[0:1, :] = jnp.sum(tile, axis=0, keepdims=True)
    group = [copy(sums_plane.at[pl.ds(0, 1)], sums_plane.at[pl.ds(i + 1, 1)], plane(o)) for i, o in enumerate(PLANE)]
    for s in group:
        s.start()
    for s in group:
        s.wait_recv()
    sums_line[0:1, :] = jnp.sum(sums_plane[...], axis=0, keepdims=True)
    group = [copy(sums_line.at[pl.ds(0, 1)], sums_line.at[pl.ds(i + 1, 1)], line(d)) for i, d in enumerate(LINE)]
    for s in group:
        s.start()
    for s in stores[:3]:
        s.start()
    for s in group:
        s.wait_recv()
    row = jnp.sum(sums_line[...], axis=0, keepdims=True)
    mine = quarter == lax.broadcasted_iota(jnp.int32, (8, W), 0)
    sums = jnp.sum(jnp.where(mine, row, 0.0), axis=1, keepdims=True)
    beta_square = sums[0:1] + EPS
    beta = jnp.sqrt(beta_square)
    inv_beta = 1.0 / beta
    alpha_next = jnp.sqrt(sums[2:3] / beta_square - 2.0 * sums[3:4] + beta_square * sums[1:2] + EPS)
    inv_alpha = 1.0 / alpha_next
    phibar, rhobar = scal[1], scal[2]
    rho = jnp.sqrt(rhobar * rhobar + beta_square)
    cosine = rhobar / rho
    sine = beta / rho
    theta = sine * alpha_next
    phi = cosine * phibar
    values = (inv_beta, inv_beta * inv_alpha, beta * inv_alpha, phi / rho, theta / rho)
    for i, value in enumerate(values):
        coef[i : i + 1, :] = jnp.broadcast_to(value, (1, W))
    coef[5:8, :] = jnp.zeros((3, W), f32)
    stores[3].start()
    for s in started:
        s.wait_send()
    for s in stores:
        s.wait()


N_COPIES = 18 + len(PLANE) + len(LINE)


def finish(
    grad_h, raw_a_h, raw_b_h, coef_h, sol_h, search_h, basis_h,
    sol_o, search_o, basis_o, resid_a_o, resid_b_o,
    grad, raw_a, raw_b, coef, sol, search, basis, load_sem, store_sem,
):
    pairs = (
        (coef_h, coef), (search_h, search), (sol_h, sol), (grad_h, grad), (basis_h, basis), (raw_a_h, raw_a), (raw_b_h, raw_b),
    )
    loads = [pltpu.make_async_copy(a, b, load_sem.at[i]) for i, (a, b) in enumerate(pairs)]
    for s in loads:
        s.start()
    pairs = ((sol, sol_o), (grad, basis_o), (search, search_o), (raw_a, resid_a_o), (raw_b, resid_b_o))
    stores = [pltpu.make_async_copy(a, b, store_sem.at[i]) for i, (a, b) in enumerate(pairs)]
    for s in loads[:3]:
        s.wait()
    inv_beta, scale, shift = coef[0:1, :], coef[1:2, :], coef[2:3, :]
    step, turn = coef[3:4, :], coef[4:5, :]
    sol[...] = sol[...] + step * search[...]
    stores[0].start()
    for s in loads[3:5]:
        s.wait()
    v = grad[...] * scale - shift * basis[...]
    grad[...] = v
    stores[1].start()
    search[...] = v - turn * search[...]
    stores[2].start()
    for s in loads[5:]:
        s.wait()
    raw_a[...] = raw_a[...] * inv_beta
    stores[3].start()
    raw_b[...] = raw_b[...] * inv_beta
    stores[4].start()
    for s in stores:
        s.wait()


def body(sol, search, basis, resid_a, resid_b, scal, pa, pb, mask, wcode, rcode):
    hbm = pl.BlockSpec(memory_space=pltpu.HBM)
    image = jax.ShapeDtypeStruct((R, W), f32)
    maps = jax.ShapeDtypeStruct((K, R, W), f32)
    words = pltpu.VMEM((R, W), jnp.int32)
    outs = pl.pallas_call(
        kernel,
        out_shape=(maps, image, image, jax.ShapeDtypeStruct((8, W), f32)),
        in_specs=[hbm] * 9,
        out_specs=(hbm,) * 4,
        scratch_shapes=[
            pltpu.VMEM((K, R, W), f32),
            pltpu.VMEM((R, W), f32),
            pltpu.VMEM((R, W), f32),
            pltpu.VMEM((8, W), f32),
            pltpu.VMEM((K, R, W), f32),
            pltpu.VMEM((R, W), f32),
            pltpu.VMEM((R, W), f32),
            pltpu.SMEM((3,), f32),
            pltpu.VMEM((K, L), f32),
            pltpu.VMEM((K, L), f32),
            words,
            words,
            words,
            pltpu.VMEM((2 * R, K * W), bf16),
            pltpu.VMEM((K * R, 2 * W), bf16),
            pltpu.VMEM((K * W, EXT), bf16),
            pltpu.VMEM((K * W, EXT), bf16),
            pltpu.VMEM((K * R, EXT), bf16),
            pltpu.VMEM((K * R, EXT), bf16),
            pltpu.VMEM((2 * R, EXT), bf16),
            pltpu.VMEM((EXT, 2 * W), bf16),
            pltpu.VMEM((5, R, W), f32),
            pltpu.VMEM((4, R, W), f32),
            pltpu.VMEM((4, R, W), f32),
            pltpu.VMEM((4, R, W), f32),
            pltpu.VMEM((R, W), f32),
            pltpu.VMEM((5, R, W), f32),
            pltpu.VMEM((4, R, W), f32),
            pltpu.VMEM((R, W), f32),
            pltpu.VMEM((5, R, W), f32),
            pltpu.VMEM((5, R, W), f32),
            pltpu.VMEM((4, R, W), f32),
            pltpu.VMEM((1 + len(PLANE), W), f32),
            pltpu.VMEM((1 + len(LINE), W), f32),
            pltpu.SemaphoreType.DMA((N_COPIES,)),
            pltpu.SemaphoreType.DMA((N_COPIES,)),
            pltpu.SemaphoreType.DMA((9,)),
        ],
        compiler_params=pltpu.CompilerParams(
            collective_id=0, has_side_effects=True, vmem_limit_bytes=56 * 1024 * 1024
        ),
    )(basis, resid_a, resid_b, scal, pa, pb, mask, wcode, rcode)
    return pl.pallas_call(
        finish,
        out_shape=(maps, maps, maps, image, image),
        in_specs=[hbm] * 7,
        out_specs=(hbm,) * 5,
        scratch_shapes=[
            pltpu.VMEM((K, R, W), f32),
            pltpu.VMEM((R, W), f32),
            pltpu.VMEM((R, W), f32),
            pltpu.VMEM((8, W), f32),
            pltpu.VMEM((K, R, W), f32),
            pltpu.VMEM((K, R, W), f32),
            pltpu.VMEM((K, R, W), f32),
            pltpu.SemaphoreType.DMA((7,)),
            pltpu.SemaphoreType.DMA((5,)),
        ],
        compiler_params=pltpu.CompilerParams(vmem_limit_bytes=56 * 1024 * 1024),
    )(*outs, sol, search, basis)


def solution(mesh):
    torus = Mesh(mesh.devices.reshape(4, 4, 2, 4, 4), (X, Z, C, H, Y))
    maps, image = P(None, ROW, COL), P(ROW, COL)
    return jax.shard_map(
        body,
        mesh=torus,
        in_specs=(maps, maps, maps, image, image, P(), P(), P(), image, image, image),
        out_specs=(maps, maps, maps, image, image),
        check_vma=False,
    )
```

time: 73.6 us -> 54.1 us (0.74)
  Pallas kernels: 64.5 us -> 53.2 us
  local copies, waits for them, and re-layouts: 7.77 us -> 0 us
    pallas_call x1, Pallas kernels: 63.6 us -> 51.1 us  [body(): pl.pallas_call(kernel, out_shape=(maps, image, image, jax.ShapeDtypeStruc...]
    unnamed x22 -> x0, local copies, waits for them, and re-layouts: 7.77 us -> none
    pallas_call x1, Pallas kernels: 0.94 us -> 2.13 us  [body(): pl.pallas_call(finish, out_shape=(maps, maps, maps, image, image), in_spe...]
where the time goes in v1:
time: 54.1 us; the launch traced here: 53.8 us
  Pallas kernels  53.2 us (98%)
  between operations  0.64 us (1%)
    pallas_call x1, Pallas kernels, body(): pl.pallas_call(kernel, out_shape=(maps, image, image, jax.ShapeDtypeStruc...  51.1 us
    pallas_call x1, Pallas kernels, body(): pl.pallas_call(finish, out_shape=(maps, maps, maps, image, image), in_spe...  2.13 us

profile of v1, /device:TPU:1, one launch (start us, length us, event | category | flops | bytes accessed | tf_op | source)
XLA Modules:
  0.0 53.8 jit_solution(5552677857429966574)
XLA Ops:
  0.6 51.1 %shard_map.146 = (f32[8,64,128]{2,1,0:T(8,128)}, f32[64,128]{1,0:T(8,128)}, f32[64,128]{1,0:T(8,128)}, f32[8,128]{1,0:T(8,128)}) custom-call(f32[8,64,128]{2,1,0:T(8,128)} %basis_h.3, f32[64,128]{1,0:T(8,128)} %resid_a_h.1, f32[64,128]{1,0:T(8,128)} %resid_b_h.1, f32[3]{0:T(128)} %scal_h.1, f32[8,512]{1,0:T(8,128)} %pa_h.1, f32[8,512]{1,0:T(8,128)} %pb_h.1, ...), custom_call_target="tpu_custom_call" | custom-call | tf_op jit(solution)/shard_map/pallas_call | solution.py:360
  51.7 2.1 %shard_map.147 = (f32[8,64,128]{2,1,0:T(8,128)}, f32[8,64,128]{2,1,0:T(8,128)}, f32[8,64,128]{2,1,0:T(8,128)}, f32[64,128]{1,0:T(8,128)}, f32[64,128]{1,0:T(8,128)}) custom-call(f32[8,64,128]{2,1,0:T(8,128)} %get-tuple-element.9.grad_h, f32[64,128]{1,0:T(8,128)} %get-tuple-element.10.raw_a_h, f32[64,128]{1,0:T(8,128)} %get-tuple-element.11.raw_b_h, ...), custom_call_target="tpu_custom_call" | custom-call | tf_op jit(solution)/shard_map/pallas_call | solution.py:408

commit v2 on v1

--- a/solution.py
+++ b/solution.py
@@ -43,7 +43,7 @@
     raw_v, raw_a, raw_b, coef, basis, resid_a, resid_b, scal, pa, pb, mask, wcode, rcode,
     src_r, src_c, ta_hi, ta_lo, tb_hi, tb_lo, wext_a, wext_b,
     even, odd, r1, r2, r3, cp, c1, c2, ext_c, ext_e, ext_o,
-    sums_plane, sums_line, send_sem, recv_sem, load_sem,
+    sums_plane, sums_line, send_sem, recv_sem, sum_sem, load_sem,
 ):
     x, z, c, h, y = (lax.axis_index(a) for a in (X, Z, C, H, Y))
     started = []
@@ -79,6 +79,19 @@
             started.append(d)
         return d
 
+    def share(sums, offsets, to, n):
+        rows = sums.at[pl.ds(0, 1)]
+        for i, o in enumerate(offsets):
+            pltpu.make_async_remote_copy(
+                src_ref=rows, dst_ref=sums.at[pl.ds(i + 1, 1)], send_sem=sum_sem.at[n], recv_sem=sum_sem.at[n + 1],
+                device_id=to(o), device_id_type=MESH,
+            ).start()
+        others = sums.at[pl.ds(1, len(offsets))]
+        return pltpu.make_async_remote_copy(
+            src_ref=others, dst_ref=others, send_sem=sum_sem.at[n], recv_sem=sum_sem.at[n + 1],
+            device_id=to(offsets[0]), device_id_type=MESH,
+        )
+
     barrier = pltpu.get_barrier_semaphore()
     peers = [core()] + [run(d) for d in (1, 2, 3)] + [along_y(d) for d in (1, 2, 3)]
     peers += [along_x(1), along_x(3), far(1), far(3)]
@@ -102,9 +115,6 @@
     loads[0].wait()
     for k in range(K):
         ta_hi[k * W : (k + 1) * W, :], ta_lo[k * W : (k + 1) * W, :] = table(pa, k, W)
-    loads[1].wait()
-    for k in range(K):
-        tb_hi[k * R : (k + 1) * R, :], tb_lo[k * R : (k + 1) * R, :] = table(pb, k, R)
 
     loads[2].wait()
     loads[3].wait()
@@ -124,6 +134,10 @@
     s_c1 = [copy(cp.at[d], c1.at[d], along_y(d)) for d in (2, 1, 3)]
     for s in s_c1:
         s.start()
+
+    loads[1].wait()
+    for k in range(K):
+        tb_hi[k * R : (k + 1) * R, :], tb_lo[k * R : (k + 1) * R, :] = table(pb, k, R)
 
     part = dot(tb_hi[...], src_c[...], 0, 0) + dot(tb_lo[...], src_c[...], 0, 0)
     part = part[:, :W] + part[:, W:]
@@ -158,7 +172,7 @@
         there = there + jnp.where(mine, 0.0, c1[d])
     cp[4] = there
     s_c2 = copy(cp.at[4], c2, far(1))
-    s_c2.start()
+    pl.when(h < 3)(s_c2.start)
 
     for s in s_r2:
         s.wait_recv()
@@ -169,16 +183,16 @@
         there = there + jnp.where(mine, 0.0, r2[d])
     even[4] = there
     s_r3 = copy(even.at[4], r3, along_x(1))
-    s_r3.start()
-
-    s_c2.wait_recv()
+    pl.when(x < 3)(s_r3.start)
+
+    pl.when(h > 0)(s_c2.wait_recv)
     image = here + jnp.where(h > 0, c2[...], 0.0)
     ra = weight_a * image - alpha * resid_a[...]
     raw_a[...] = ra
     wa = weight_a * ra
     ext_c[0] = wa
     s_d1 = copy(ext_c.at[0], ext_c.at[4], far(3))
-    s_d1.start()
+    pl.when(h > 0)(s_d1.start)
     s_d2 = []
     for d in (1, 2, 3):
         to = along_y(d)
@@ -188,14 +202,14 @@
     for s, later, now in s_d2:
         pl.when(now)(s.start)
 
-    s_r3.wait_recv()
+    pl.when(x > 0)(s_r3.wait_recv)
     image = rows_here + jnp.where(x > 0, r3[...], 0.0)
     rb = weight_b * image - alpha * resid_b[...]
     raw_b[...] = rb
     wb = weight_b * rb
     ext_e[0] = wb
     s_a1 = copy(ext_e.at[0], ext_e.at[4], along_x(3))
-    s_a1.start()
+    pl.when(x > 0)(s_a1.start)
     s_a2 = []
     for d in (1, 2, 3):
         to = run(d)
@@ -216,13 +230,13 @@
         sq = sq + basis[k] * basis[k]
     vv = tile_of(sq)
 
-    s_d1.wait_recv()
+    pl.when(x < 3)(s_a1.wait_recv)
+    ext_e[4] = jnp.where(x < 3, ext_e[4], 0.0)
+    for s, later, now in s_a2:
+        pl.when(jnp.logical_not(now))(later.start)
+    pl.when(h < 3)(s_d1.wait_recv)
     ext_c[4] = jnp.where(h < 3, ext_c[4], 0.0)
     for s, later, now in s_d2:
-        pl.when(jnp.logical_not(now))(later.start)
-    s_a1.wait_recv()
-    ext_e[4] = jnp.where(x < 3, ext_e[4], 0.0)
-    for s, later, now in s_a2:
         pl.when(jnp.logical_not(now))(later.start)
 
     def put_a(level, block):
@@ -241,29 +255,36 @@
     put_b(8, ext_e[4])
     put_b(9, jnp.zeros((R, W), f32))
 
+    ends = wext_a[:, :W], wext_a[:, EXT - W :]
+    tables = ta_hi, ta_lo
+    ga = sum(dot(w, t[:, at], 1, 1) for t in tables for w, at in zip(ends, (slice(0, W), slice(EXT - W, EXT))))
+    ga = ga[:R] + ga[R:]
+    for k in range(K):
+        raw_v[k] = ga[:, k * W : (k + 1) * W]
     for s, _, _ in s_a2:
         s.wait_recv()
     s_a3 = copy(ext_e.at[pl.ds(1 - c, 4)], ext_o, core())
     s_a3.start()
     for d in (1, 2, 3):
         put_b(2 * d, ext_e[d])
-    for s, _, _ in s_d2:
-        s.wait_recv()
-    for d in (1, 2, 3):
-        put_a(d, ext_c[d])
-    ga = dot(wext_a[...], ta_hi[...], 1, 1) + dot(wext_a[...], ta_lo[...], 1, 1)
-    ga = ga[:R] + ga[R:]
-    for k in range(K):
-        raw_v[k] = ga[:, k * W : (k + 1) * W]
     s_a3.wait_recv()
     for d in range(4):
         put_b(2 * d + 1, ext_o[d])
     gb = dot(tb_hi[...], wext_b[...], 1, 0) + dot(tb_lo[...], wext_b[...], 1, 0)
     gb = gb[:, :W] + gb[:, W:]
+    for k in range(K):
+        raw_v[k] = raw_v[k] + gb[k * R : (k + 1) * R]
+    for s, _, _ in s_d2:
+        s.wait_recv()
+    for d in (1, 2, 3):
+        put_a(d, ext_c[d])
+    middle = slice(W, EXT - W)
+    ga = dot(wext_a[:, middle], ta_hi[:, middle], 1, 1) + dot(wext_a[:, middle], ta_lo[:, middle], 1, 1)
+    ga = ga[:R] + ga[R:]
     zz = jnp.zeros((R, W), f32)
     zv = jnp.zeros((R, W), f32)
     for k in range(K):
-        g = m * (raw_v[k] + gb[k * R : (k + 1) * R])
+        g = m * (raw_v[k] + ga[:, k * W : (k + 1) * W])
         raw_v[k] = g
         zz = zz + g * g
         zv = zv + g * basis[k]
@@ -275,19 +296,19 @@
     both = jnp.where(quarter == 0, rr, vv)
     tile = jnp.where(quarter == 2, tile_of(zz), jnp.where(quarter == 3, tile_of(zv), both))
     sums_plane[0:1, :] = jnp.sum(tile, axis=0, keepdims=True)
-    group = [copy(sums_plane.at[pl.ds(0, 1)], sums_plane.at[pl.ds(i + 1, 1)], plane(o)) for i, o in enumerate(PLANE)]
-    for s in group:
-        s.start()
-    for s in group:
-        s.wait_recv()
-    sums_line[0:1, :] = jnp.sum(sums_plane[...], axis=0, keepdims=True)
-    group = [copy(sums_line.at[pl.ds(0, 1)], sums_line.at[pl.ds(i + 1, 1)], line(d)) for i, d in enumerate(LINE)]
-    for s in group:
-        s.start()
+    group_plane = share(sums_plane, PLANE, plane, 0)
     for s in stores[:3]:
         s.start()
-    for s in group:
-        s.wait_recv()
+    sent = {id(s_c2): h < 3, id(s_r3): x < 3, id(s_d1): h > 0, id(s_a1): x > 0}
+    for s in started:
+        pl.when(sent.get(id(s), True))(s.wait_send)
+    group_plane.wait_recv()
+    sums_line[0:1, :] = jnp.sum(sums_plane[...], axis=0, keepdims=True)
+    group_line = share(sums_line, LINE, line, 2)
+    group_plane.wait_send()
+    for s in stores[:3]:
+        s.wait()
+    group_line.wait_recv()
     row = jnp.sum(sums_line[...], axis=0, keepdims=True)
     mine = quarter == lax.broadcasted_iota(jnp.int32, (8, W), 0)
     sums = jnp.sum(jnp.where(mine, row, 0.0), axis=1, keepdims=True)
@@ -307,13 +328,11 @@
         coef[i : i + 1, :] = jnp.broadcast_to(value, (1, W))
     coef[5:8, :] = jnp.zeros((3, W), f32)
     stores[3].start()
-    for s in started:
-        s.wait_send()
-    for s in stores:
-        s.wait()
-
-
-N_COPIES = 18 + len(PLANE) + len(LINE)
+    group_line.wait_send()
+    stores[3].wait()
+
+
+N_COPIES = 18
 
 
 def finish(
@@ -399,6 +418,7 @@
             pltpu.VMEM((1 + len(LINE), W), f32),
             pltpu.SemaphoreType.DMA((N_COPIES,)),
             pltpu.SemaphoreType.DMA((N_COPIES,)),
+            pltpu.SemaphoreType.DMA((4,)),
             pltpu.SemaphoreType.DMA((9,)),
         ],
         compiler_params=pltpu.CompilerParams(

time: 54.1 us -> 51.1 us (0.945)
  Pallas kernels: 53.2 us -> 50.2 us
    pallas_call x1, Pallas kernels: 51.1 us -> 48 us  [body(): pl.pallas_call(kernel, out_shape=(maps, image, image, jax.ShapeDtypeStruc...]
where the time goes in v2:
time: 51.1 us; the launch traced here: 50.8 us
  Pallas kernels  50.2 us (98%)
  between operations  0.64 us (1%)
    pallas_call x1, Pallas kernels, body(): pl.pallas_call(kernel, out_shape=(maps, image, image, jax.ShapeDtypeStruc...  48 us
    pallas_call x1, Pallas kernels, body(): pl.pallas_call(finish, out_shape=(maps, maps, maps, image, image), in_spe...  2.13 us

profile of v2, /device:TPU:1, one launch (start us, length us, event | category | flops | bytes accessed | tf_op | source)
XLA Modules:
  0.0 50.8 jit_solution(10896993797585743673)
XLA Ops:
  0.6 48.0 %shard_map.146 = (f32[8,64,128]{2,1,0:T(8,128)}, f32[64,128]{1,0:T(8,128)}, f32[64,128]{1,0:T(8,128)}, f32[8,128]{1,0:T(8,128)}) custom-call(f32[8,64,128]{2,1,0:T(8,128)} %basis_h.3, f32[64,128]{1,0:T(8,128)} %resid_a_h.1, f32[64,128]{1,0:T(8,128)} %resid_b_h.1, f32[3]{0:T(128)} %scal_h.1, f32[8,512]{1,0:T(8,128)} %pa_h.1, f32[8,512]{1,0:T(8,128)} %pb_h.1, ...), custom_call_target="tpu_custom_call" | custom-call | tf_op jit(solution)/shard_map/pallas_call | solution.py:379
  48.7 2.1 %shard_map.147 = (f32[8,64,128]{2,1,0:T(8,128)}, f32[8,64,128]{2,1,0:T(8,128)}, f32[8,64,128]{2,1,0:T(8,128)}, f32[64,128]{1,0:T(8,128)}, f32[64,128]{1,0:T(8,128)}) custom-call(f32[8,64,128]{2,1,0:T(8,128)} %get-tuple-element.9.grad_h, f32[64,128]{1,0:T(8,128)} %get-tuple-element.10.raw_a_h, f32[64,128]{1,0:T(8,128)} %get-tuple-element.11.raw_b_h, ...), custom_call_target="tpu_custom_call" | custom-call | tf_op jit(solution)/shard_map/pallas_call | solution.py:428

commit v3 on v2

--- a/solution.py
+++ b/solution.py
@@ -43,7 +43,8 @@
     raw_v, raw_a, raw_b, coef, basis, resid_a, resid_b, scal, pa, pb, mask, wcode, rcode,
     src_r, src_c, ta_hi, ta_lo, tb_hi, tb_lo, wext_a, wext_b,
     even, odd, r1, r2, r3, cp, c1, c2, ext_c, ext_e, ext_o,
-    sums_plane, sums_line, send_sem, recv_sem, sum_sem, load_sem,
+    sums_plane, sums_line, send_sem, recv_sem, sum_sem, load_sem, ready,
+    square_a, square_b, next_square_a, next_square_b, next_a, next_b,
 ):
     x, z, c, h, y = (lax.axis_index(a) for a in (X, Z, C, H, Y))
     started = []
@@ -126,15 +127,21 @@
         src_c[k * R : (k + 1) * R, 0:W] = hi
         src_c[k * R : (k + 1) * R, W : 2 * W] = lo
 
-    part = dot(src_r[...], ta_hi[...], 1, 0) + dot(src_r[...], ta_lo[...], 1, 0)
+    middle = slice(W, EXT - W)
+    part = dot(src_r[...], ta_hi[:, middle], 1, 0) + dot(src_r[...], ta_lo[:, middle], 1, 0)
     part = part[:R] + part[R:]
-    for level in range(CL):
-        cp[level] = part[:, level * W : (level + 1) * W]
-    pl.semaphore_wait(barrier, len(peers))
-    s_c1 = [copy(cp.at[d], c1.at[d], along_y(d)) for d in (2, 1, 3)]
-    for s in s_c1:
-        s.start()
-
+    for level in (1, 2, 3):
+        cp[level] = part[:, (level - 1) * W : level * W]
+    for level in (0, 4):
+        at = slice(level * W, (level + 1) * W)
+        part = dot(src_r[...], ta_hi[:, at], 1, 0) + dot(src_r[...], ta_lo[:, at], 1, 0)
+        cp[level] = part[:R] + part[R:]
+    for s in loads[4:]:
+        s.wait()
+    alpha = scal[0]
+    base = 1.0 / (1.0 + 0.25 * wcode[...].astype(f32))
+    weight_a = jnp.where(rcode[...] != 2, base, 0.0)
+    weight_b = jnp.where(rcode[...] != 1, base, 0.0)
     loads[1].wait()
     for k in range(K):
         tb_hi[k * R : (k + 1) * R, :], tb_lo[k * R : (k + 1) * R, :] = table(pb, k, R)
@@ -147,14 +154,19 @@
             odd[level // 2] = block
         else:
             even[level // 2] = block
+    square_a[...] = weight_a * weight_a
+    square_b[...] = weight_b * weight_b
+
+    pl.semaphore_wait(barrier, len(peers))
     s_r1 = copy(odd, r1, core())
     s_r1.start()
-    for s in loads[4:]:
-        s.wait()
-    alpha = scal[0]
-    base = 1.0 / (1.0 + 0.25 * wcode[...].astype(f32))
-    weight_a = jnp.where(rcode[...] != 2, base, 0.0)
-    weight_b = jnp.where(rcode[...] != 1, base, 0.0)
+    s_c1 = [copy(cp.at[d], c1.at[d], along_y(d)) for d in (2, 1, 3)]
+    for s in s_c1:
+        s.start()
+    s_k1 = copy(square_a, next_square_a, far(3))
+    pl.when(h > 0)(s_k1.start)
+    s_k2 = copy(square_b, next_square_b, along_x(3))
+    pl.when(x > 0)(s_k2.start)
 
     s_r1.wait_recv()
     for i in range(4):
@@ -170,9 +182,14 @@
         mine = d <= y
         here = here + jnp.where(mine, c1[d], 0.0)
         there = there + jnp.where(mine, 0.0, c1[d])
+    beyond = there
     cp[4] = there
     s_c2 = copy(cp.at[4], c2, far(1))
     pl.when(h < 3)(s_c2.start)
+    part_a = weight_a * (weight_a * here - alpha * resid_a[...])
+    cp[0] = part_a
+    s_d1 = copy(cp.at[0], next_a, far(3))
+    pl.when(h > 0)(s_d1.start)
 
     for s in s_r2:
         s.wait_recv()
@@ -184,15 +201,35 @@
     even[4] = there
     s_r3 = copy(even.at[4], r3, along_x(1))
     pl.when(x < 3)(s_r3.start)
+    part_b = weight_b * (weight_b * rows_here - alpha * resid_b[...])
+    even[0] = part_b
+    s_a1 = copy(even.at[0], next_b, along_x(3))
+    pl.when(x > 0)(s_a1.start)
+
+    pl.when(x > 0)(s_r3.wait_recv)
+    came = jnp.where(x > 0, r3[...], 0.0)
+    wb = part_b + square_b[...] * came
+    ext_e[0] = wb
+    s_a2 = []
+    for d in (1, 2, 3):
+        to = run(d)
+        s = copy(ext_e.at[0], ext_e.at[4 - d], to)
+        later = copy(ext_e.at[4], ext_e.at[4 - d], to, again=True)
+        s_a2.append((s, later, z + d >= 4))
+    for s, later, now in s_a2:
+        pl.when(now)(s.start)
+    rb = weight_b * (rows_here + came) - alpha * resid_b[...]
+    raw_b[...] = rb
+    pl.when(x < 3)(s_k2.wait_recv)
+    pl.when(x < 3)(s_a1.wait_recv)
+    ext_e[4] = jnp.where(x < 3, next_b[...] + next_square_b[...] * there, 0.0)
+    for s, later, now in s_a2:
+        pl.when(jnp.logical_not(now))(later.start)
 
     pl.when(h > 0)(s_c2.wait_recv)
-    image = here + jnp.where(h > 0, c2[...], 0.0)
-    ra = weight_a * image - alpha * resid_a[...]
-    raw_a[...] = ra
-    wa = weight_a * ra
+    came = jnp.where(h > 0, c2[...], 0.0)
+    wa = part_a + square_a[...] * came
     ext_c[0] = wa
-    s_d1 = copy(ext_c.at[0], ext_c.at[4], far(3))
-    pl.when(h > 0)(s_d1.start)
     s_d2 = []
     for d in (1, 2, 3):
         to = along_y(d)
@@ -201,23 +238,15 @@
         s_d2.append((s, later, y + d >= 4))
     for s, later, now in s_d2:
         pl.when(now)(s.start)
-
-    pl.when(x > 0)(s_r3.wait_recv)
-    image = rows_here + jnp.where(x > 0, r3[...], 0.0)
-    rb = weight_b * image - alpha * resid_b[...]
-    raw_b[...] = rb
-    wb = weight_b * rb
-    ext_e[0] = wb
-    s_a1 = copy(ext_e.at[0], ext_e.at[4], along_x(3))
-    pl.when(x > 0)(s_a1.start)
-    s_a2 = []
-    for d in (1, 2, 3):
-        to = run(d)
-        s = copy(ext_e.at[0], ext_e.at[4 - d], to)
-        later = copy(ext_e.at[4], ext_e.at[4 - d], to, again=True)
-        s_a2.append((s, later, z + d >= 4))
-    for s, later, now in s_a2:
-        pl.when(now)(s.start)
+    ra = weight_a * (here + came) - alpha * resid_a[...]
+    raw_a[...] = ra
+    pl.when(h < 3)(s_k1.wait_recv)
+    pl.when(h < 3)(s_d1.wait_recv)
+    ext_c[4] = jnp.where(h < 3, next_a[...] + next_square_a[...] * beyond, 0.0)
+    for s, later, now in s_d2:
+        pl.when(jnp.logical_not(now))(later.start)
+    for d in (1, 2, 3):
+        pl.semaphore_signal(ready, inc=1, device_id=run(d), device_id_type=MESH)
 
     def tile_of(q):
         t = jnp.sum(q.reshape(-1, 8, W), axis=0)
@@ -229,15 +258,6 @@
     for k in range(K):
         sq = sq + basis[k] * basis[k]
     vv = tile_of(sq)
-
-    pl.when(x < 3)(s_a1.wait_recv)
-    ext_e[4] = jnp.where(x < 3, ext_e[4], 0.0)
-    for s, later, now in s_a2:
-        pl.when(jnp.logical_not(now))(later.start)
-    pl.when(h < 3)(s_d1.wait_recv)
-    ext_c[4] = jnp.where(h < 3, ext_c[4], 0.0)
-    for s, later, now in s_d2:
-        pl.when(jnp.logical_not(now))(later.start)
 
     def put_a(level, block):
         hi, lo = split(block)
@@ -267,24 +287,23 @@
     s_a3.start()
     for d in (1, 2, 3):
         put_b(2 * d, ext_e[d])
+    for s, _, _ in s_d2:
+        s.wait_recv()
+    for d in (1, 2, 3):
+        put_a(d, ext_c[d])
+    ga = dot(wext_a[:, middle], ta_hi[:, middle], 1, 1) + dot(wext_a[:, middle], ta_lo[:, middle], 1, 1)
+    ga = ga[:R] + ga[R:]
+    for k in range(K):
+        raw_v[k] = raw_v[k] + ga[:, k * W : (k + 1) * W]
     s_a3.wait_recv()
     for d in range(4):
         put_b(2 * d + 1, ext_o[d])
     gb = dot(tb_hi[...], wext_b[...], 1, 0) + dot(tb_lo[...], wext_b[...], 1, 0)
     gb = gb[:, :W] + gb[:, W:]
-    for k in range(K):
-        raw_v[k] = raw_v[k] + gb[k * R : (k + 1) * R]
-    for s, _, _ in s_d2:
-        s.wait_recv()
-    for d in (1, 2, 3):
-        put_a(d, ext_c[d])
-    middle = slice(W, EXT - W)
-    ga = dot(wext_a[:, middle], ta_hi[:, middle], 1, 1) + dot(wext_a[:, middle], ta_lo[:, middle], 1, 1)
-    ga = ga[:R] + ga[R:]
     zz = jnp.zeros((R, W), f32)
     zv = jnp.zeros((R, W), f32)
     for k in range(K):
-        g = m * (raw_v[k] + ga[:, k * W : (k + 1) * W])
+        g = m * (raw_v[k] + gb[k * R : (k + 1) * R])
         raw_v[k] = g
         zz = zz + g * g
         zv = zv + g * basis[k]
@@ -299,11 +318,12 @@
     group_plane = share(sums_plane, PLANE, plane, 0)
     for s in stores[:3]:
         s.start()
-    sent = {id(s_c2): h < 3, id(s_r3): x < 3, id(s_d1): h > 0, id(s_a1): x > 0}
+    sent = {id(s_c2): h < 3, id(s_r3): x < 3, id(s_d1): h > 0, id(s_a1): x > 0, id(s_k1): h > 0, id(s_k2): x > 0}
     for s in started:
         pl.when(sent.get(id(s), True))(s.wait_send)
     group_plane.wait_recv()
     sums_line[0:1, :] = jnp.sum(sums_plane[...], axis=0, keepdims=True)
+    pl.semaphore_wait(ready, 3)
     group_line = share(sums_line, LINE, line, 2)
     group_plane.wait_send()
     for s in stores[:3]:
@@ -312,18 +332,16 @@
     row = jnp.sum(sums_line[...], axis=0, keepdims=True)
     mine = quarter == lax.broadcasted_iota(jnp.int32, (8, W), 0)
     sums = jnp.sum(jnp.where(mine, row, 0.0), axis=1, keepdims=True)
+    phibar, rhobar = scal[1], scal[2]
     beta_square = sums[0:1] + EPS
-    beta = jnp.sqrt(beta_square)
-    inv_beta = 1.0 / beta
-    alpha_next = jnp.sqrt(sums[2:3] / beta_square - 2.0 * sums[3:4] + beta_square * sums[1:2] + EPS)
-    inv_alpha = 1.0 / alpha_next
-    phibar, rhobar = scal[1], scal[2]
-    rho = jnp.sqrt(rhobar * rhobar + beta_square)
-    cosine = rhobar / rho
-    sine = beta / rho
-    theta = sine * alpha_next
-    phi = cosine * phibar
-    values = (inv_beta, inv_beta * inv_alpha, beta * inv_alpha, phi / rho, theta / rho)
+    inv_beta = lax.rsqrt(beta_square)
+    inv_rho_square = 1.0 / (rhobar * rhobar + beta_square)
+    beta = beta_square * inv_beta
+    alpha_square = sums[2:3] * (inv_beta * inv_beta) - 2.0 * sums[3:4] + beta_square * sums[1:2] + EPS
+    inv_alpha = lax.rsqrt(alpha_square)
+    alpha_next = alpha_square * inv_alpha
+    step = rhobar * phibar * inv_rho_square
+    values = (inv_beta, inv_beta * inv_alpha, beta * inv_alpha, step, beta * alpha_next * inv_rho_square)
     for i, value in enumerate(values):
         coef[i : i + 1, :] = jnp.broadcast_to(value, (1, W))
     coef[5:8, :] = jnp.zeros((3, W), f32)
@@ -332,7 +350,7 @@
     stores[3].wait()
 
 
-N_COPIES = 18
+N_COPIES = 20
 
 
 def finish(
@@ -420,6 +438,8 @@
             pltpu.SemaphoreType.DMA((N_COPIES,)),
             pltpu.SemaphoreType.DMA((4,)),
             pltpu.SemaphoreType.DMA((9,)),
+            pltpu.SemaphoreType.REGULAR,
+            *[pltpu.VMEM((R, W), f32)] * 6,
         ],
         compiler_params=pltpu.CompilerParams(
             collective_id=0, has_side_effects=True, vmem_limit_bytes=56 * 1024 * 1024

time: 51.1 us -> 48.5 us (0.949)
  Pallas kernels: 50.2 us -> 47.6 us
    pallas_call x1, Pallas kernels: 48 us -> 45.5 us  [body(): pl.pallas_call(kernel, out_shape=(maps, image, image, jax.ShapeDtypeStruc...]
where the time goes in v3:
time: 48.5 us; the launch traced here: 48.3 us
  Pallas kernels  47.6 us (98%)
  between operations  0.64 us (1%)
    pallas_call x1, Pallas kernels, body(): pl.pallas_call(kernel, out_shape=(maps, image, image, jax.ShapeDtypeStruc...  45.5 us
    pallas_call x1, Pallas kernels, body(): pl.pallas_call(finish, out_shape=(maps, maps, maps, image, image), in_spe...  2.13 us

profile of v3, /device:TPU:1, one launch (start us, length us, event | category | flops | bytes accessed | tf_op | source)
XLA Modules:
  0.0 48.3 jit_solution(7096970103769084757)
XLA Ops:
  0.6 45.5 %shard_map.146 = (f32[8,64,128]{2,1,0:T(8,128)}, f32[64,128]{1,0:T(8,128)}, f32[64,128]{1,0:T(8,128)}, f32[8,128]{1,0:T(8,128)}) custom-call(f32[8,64,128]{2,1,0:T(8,128)} %basis_h.3, f32[64,128]{1,0:T(8,128)} %resid_a_h.1, f32[64,128]{1,0:T(8,128)} %resid_b_h.1, f32[3]{0:T(128)} %scal_h.1, f32[8,512]{1,0:T(8,128)} %pa_h.1, f32[8,512]{1,0:T(8,128)} %pb_h.1, ...), custom_call_target="tpu_custom_call" | custom-call | tf_op jit(solution)/shard_map/pallas_call | solution.py:397
  46.1 2.1 %shard_map.147 = (f32[8,64,128]{2,1,0:T(8,128)}, f32[8,64,128]{2,1,0:T(8,128)}, f32[8,64,128]{2,1,0:T(8,128)}, f32[64,128]{1,0:T(8,128)}, f32[64,128]{1,0:T(8,128)}) custom-call(f32[8,64,128]{2,1,0:T(8,128)} %get-tuple-element.9.grad_h, f32[64,128]{1,0:T(8,128)} %get-tuple-element.10.raw_a_h, f32[64,128]{1,0:T(8,128)} %get-tuple-element.11.raw_b_h, ...), custom_call_target="tpu_custom_call" | custom-call | tf_op jit(solution)/shard_map/pallas_call | solution.py:448

commit v4 on v3

--- a/solution.py
+++ b/solution.py
@@ -41,10 +41,10 @@
     basis_h, resid_a_h, resid_b_h, scal_h, pa_h, pb_h, mask_h, wcode_h, rcode_h,
     raw_v_h, raw_a_h, raw_b_h, coef_h,
     raw_v, raw_a, raw_b, coef, basis, resid_a, resid_b, scal, pa, pb, mask, wcode, rcode,
-    src_r, src_c, ta_hi, ta_lo, tb_hi, tb_lo, wext_a, wext_b,
+    src_r, src_c, ta_hi, ta_lo, tb_hi, tb_lo, to_hi, to_lo, wext_a, wext_b, wext_o,
     even, odd, r1, r2, r3, cp, c1, c2, ext_c, ext_e, ext_o,
     sums_plane, sums_line, send_sem, recv_sem, sum_sem, load_sem, ready,
-    square_a, square_b, next_square_a, next_square_b, next_a, next_b,
+    square_a, next_square_a, next_a,
 ):
     x, z, c, h, y = (lax.axis_index(a) for a in (X, Z, C, H, Y))
     started = []
@@ -54,6 +54,9 @@
 
     def run(d):
         return {Z: lax.rem(z + d, 4)}
+
+    def across(d):
+        return {Z: lax.rem(z + d, 4), X: lax.rem(x + jnp.where(z + d < 4, 3, 1), 4)}
 
     def along_x(d):
         return {X: lax.rem(x + d, 4)}
@@ -94,7 +97,7 @@
         )
 
     barrier = pltpu.get_barrier_semaphore()
-    peers = [core()] + [run(d) for d in (1, 2, 3)] + [along_y(d) for d in (1, 2, 3)]
+    peers = [core()] + [run(d) for d in (1, 2, 3)] + [across(d) for d in (1, 2, 3)] + [along_y(d) for d in (1, 2, 3)]
     peers += [along_x(1), along_x(3), far(1), far(3)]
     for to in peers:
         pl.semaphore_signal(barrier, inc=1, device_id=to, device_id_type=MESH)
@@ -144,7 +147,11 @@
     weight_b = jnp.where(rcode[...] != 1, base, 0.0)
     loads[1].wait()
     for k in range(K):
-        tb_hi[k * R : (k + 1) * R, :], tb_lo[k * R : (k + 1) * R, :] = table(pb, k, R)
+        at = slice(k * R, (k + 1) * R)
+        hi, lo = table(pb, k, R)
+        tb_hi[at, :], tb_lo[at, :] = hi, lo
+        for source, dest in ((hi, to_hi), (lo, to_lo)):
+            dest[at, :] = jnp.concatenate([source[:, (2 * i + 1) * R : (2 * i + 2) * R] for i in range(4)], axis=1)
 
     part = dot(tb_hi[...], src_c[...], 0, 0) + dot(tb_lo[...], src_c[...], 0, 0)
     part = part[:, :W] + part[:, W:]
@@ -155,7 +162,6 @@
         else:
             even[level // 2] = block
     square_a[...] = weight_a * weight_a
-    square_b[...] = weight_b * weight_b
 
     pl.semaphore_wait(barrier, len(peers))
     s_r1 = copy(odd, r1, core())
@@ -165,15 +171,20 @@
         s.start()
     s_k1 = copy(square_a, next_square_a, far(3))
     pl.when(h > 0)(s_k1.start)
-    s_k2 = copy(square_b, next_square_b, along_x(3))
-    pl.when(x > 0)(s_k2.start)
 
     s_r1.wait_recv()
     for i in range(4):
         even[1 - c + i] = even[1 - c + i] + r1[i]
-    s_r2 = [copy(even.at[d], r2.at[d], run(d)) for d in (1, 2, 3)]
-    for s in s_r2:
-        s.start()
+    s_r2 = []
+    for d in (1, 2, 3):
+        inside = z + d < 4
+        near = copy(even.at[d], r2.at[d], run(d))
+        cross = copy(even.at[d], r2.at[d], across(d), again=True)
+        pl.when(inside)(near.start)
+        pl.when(jnp.logical_not(inside) & (x < 3))(cross.start)
+        s_r2.append((near, (d <= z) | (x > 0), inside | (x < 3)))
+    s_r3 = copy(even.at[4], r3, along_x(1))
+    pl.when(x < 3)(s_r3.start)
 
     for s in s_c1:
         s.wait_recv()
@@ -191,40 +202,26 @@
     s_d1 = copy(cp.at[0], next_a, far(3))
     pl.when(h > 0)(s_d1.start)
 
-    for s in s_r2:
-        s.wait_recv()
-    rows_here, there = even[0], even[4]
-    for d in (1, 2, 3):
-        mine = d <= z
-        rows_here = rows_here + jnp.where(mine, r2[d], 0.0)
-        there = there + jnp.where(mine, 0.0, r2[d])
-    even[4] = there
-    s_r3 = copy(even.at[4], r3, along_x(1))
-    pl.when(x < 3)(s_r3.start)
-    part_b = weight_b * (weight_b * rows_here - alpha * resid_b[...])
-    even[0] = part_b
-    s_a1 = copy(even.at[0], next_b, along_x(3))
-    pl.when(x > 0)(s_a1.start)
-
+    rows_here = even[0]
+    for d, (s, comes, _) in enumerate(s_r2, 1):
+        pl.when(comes)(s.wait_recv)
+        rows_here = rows_here + jnp.where(comes, r2[d], 0.0)
     pl.when(x > 0)(s_r3.wait_recv)
-    came = jnp.where(x > 0, r3[...], 0.0)
-    wb = part_b + square_b[...] * came
+    rows_here = rows_here + jnp.where(x > 0, r3[...], 0.0)
+    rb = weight_b * rows_here - alpha * resid_b[...]
+    wb = weight_b * rb
     ext_e[0] = wb
     s_a2 = []
-    for d in (1, 2, 3):
-        to = run(d)
-        s = copy(ext_e.at[0], ext_e.at[4 - d], to)
-        later = copy(ext_e.at[4], ext_e.at[4 - d], to, again=True)
-        s_a2.append((s, later, z + d >= 4))
-    for s, later, now in s_a2:
-        pl.when(now)(s.start)
-    rb = weight_b * (rows_here + came) - alpha * resid_b[...]
+    for d in (3, 2, 1):
+        inside = z + d >= 4
+        near = copy(ext_e.at[0], ext_e.at[4 - d], run(d))
+        cross = copy(ext_e.at[0], ext_e.at[4 - d], across(d), again=True)
+        pl.when(inside)(near.start)
+        pl.when(jnp.logical_not(inside) & (x > 0))(cross.start)
+        s_a2.append((near, (z + 4 - d < 4) | (x < 3), inside | (x > 0)))
+    s_a1 = copy(ext_e.at[0], ext_e.at[4], along_x(3))
+    pl.when(x > 0)(s_a1.start)
     raw_b[...] = rb
-    pl.when(x < 3)(s_k2.wait_recv)
-    pl.when(x < 3)(s_a1.wait_recv)
-    ext_e[4] = jnp.where(x < 3, next_b[...] + next_square_b[...] * there, 0.0)
-    for s, later, now in s_a2:
-        pl.when(jnp.logical_not(now))(later.start)
 
     pl.when(h > 0)(s_c2.wait_recv)
     came = jnp.where(h > 0, c2[...], 0.0)
@@ -272,8 +269,8 @@
     put_a(0, wa)
     put_a(4, ext_c[4])
     put_b(0, wb)
-    put_b(8, ext_e[4])
-    put_b(9, jnp.zeros((R, W), f32))
+    for level in (1, 3, 5, 7, 9):
+        wext_b[level * R : (level + 1) * R, :] = jnp.zeros((R, 2 * W), bf16)
 
     ends = wext_a[:, :W], wext_a[:, EXT - W :]
     tables = ta_hi, ta_lo
@@ -281,12 +278,19 @@
     ga = ga[:R] + ga[R:]
     for k in range(K):
         raw_v[k] = ga[:, k * W : (k + 1) * W]
-    for s, _, _ in s_a2:
-        s.wait_recv()
+    for level, (s, comes, _) in enumerate(s_a2, 1):
+        pl.when(comes)(s.wait_recv)
+        ext_e[level] = jnp.where(comes, ext_e[level], 0.0)
+    pl.when(x < 3)(s_a1.wait_recv)
+    ext_e[4] = jnp.where(x < 3, ext_e[4], 0.0)
     s_a3 = copy(ext_e.at[pl.ds(1 - c, 4)], ext_o, core())
     s_a3.start()
-    for d in (1, 2, 3):
+    for d in (1, 2, 3, 4):
         put_b(2 * d, ext_e[d])
+    gb = dot(tb_hi[...], wext_b[...], 1, 0) + dot(tb_lo[...], wext_b[...], 1, 0)
+    gb = gb[:, :W] + gb[:, W:]
+    for k in range(K):
+        raw_v[k] = raw_v[k] + gb[k * R : (k + 1) * R]
     for s, _, _ in s_d2:
         s.wait_recv()
     for d in (1, 2, 3):
@@ -297,8 +301,10 @@
         raw_v[k] = raw_v[k] + ga[:, k * W : (k + 1) * W]
     s_a3.wait_recv()
     for d in range(4):
-        put_b(2 * d + 1, ext_o[d])
-    gb = dot(tb_hi[...], wext_b[...], 1, 0) + dot(tb_lo[...], wext_b[...], 1, 0)
+        hi, lo = split(ext_o[d])
+        wext_o[d * R : (d + 1) * R, 0:W] = hi
+        wext_o[d * R : (d + 1) * R, W : 2 * W] = lo
+    gb = dot(to_hi[...], wext_o[...], 1, 0) + dot(to_lo[...], wext_o[...], 1, 0)
     gb = gb[:, :W] + gb[:, W:]
     zz = jnp.zeros((R, W), f32)
     zv = jnp.zeros((R, W), f32)
@@ -318,7 +324,8 @@
     group_plane = share(sums_plane, PLANE, plane, 0)
     for s in stores[:3]:
         s.start()
-    sent = {id(s_c2): h < 3, id(s_r3): x < 3, id(s_d1): h > 0, id(s_a1): x > 0, id(s_k1): h > 0, id(s_k2): x > 0}
+    sent = {id(s_c2): h < 3, id(s_r3): x < 3, id(s_d1): h > 0, id(s_a1): x > 0, id(s_k1): h > 0}
+    sent.update((id(s), goes) for s, _, goes in s_r2 + s_a2)
     for s in started:
         pl.when(sent.get(id(s), True))(s.wait_send)
     group_plane.wait_recv()
@@ -350,7 +357,7 @@
     stores[3].wait()
 
 
-N_COPIES = 20
+N_COPIES = 19
 
 
 def finish(
@@ -419,8 +426,11 @@
             pltpu.VMEM((K * W, EXT), bf16),
             pltpu.VMEM((K * R, EXT), bf16),
             pltpu.VMEM((K * R, EXT), bf16),
+            pltpu.VMEM((K * R, 4 * R), bf16),
+            pltpu.VMEM((K * R, 4 * R), bf16),
             pltpu.VMEM((2 * R, EXT), bf16),
             pltpu.VMEM((EXT, 2 * W), bf16),
+            pltpu.VMEM((4 * R, 2 * W), bf16),
             pltpu.VMEM((5, R, W), f32),
             pltpu.VMEM((4, R, W), f32),
             pltpu.VMEM((4, R, W), f32),
@@ -439,7 +449,7 @@
             pltpu.SemaphoreType.DMA((4,)),
             pltpu.SemaphoreType.DMA((9,)),
             pltpu.SemaphoreType.REGULAR,
-            *[pltpu.VMEM((R, W), f32)] * 6,
+            *[pltpu.VMEM((R, W), f32)] * 3,
         ],
         compiler_params=pltpu.CompilerParams(
             collective_id=0, has_side_effects=True, vmem_limit_bytes=56 * 1024 * 1024

time: 48.5 us -> 46.8 us (0.965)
  Pallas kernels: 47.6 us -> 45.9 us
    pallas_call x1, Pallas kernels: 45.5 us -> 43.7 us  [body(): pl.pallas_call(kernel, out_shape=(maps, image, image, jax.ShapeDtypeStruc...]
where the time goes in v4:
time: 46.8 us; the launch traced here: 46.5 us
  Pallas kernels  45.9 us (98%)
  between operations  0.64 us (1%)
    pallas_call x1, Pallas kernels, body(): pl.pallas_call(kernel, out_shape=(maps, image, image, jax.ShapeDtypeStruc...  43.7 us
    pallas_call x1, Pallas kernels, body(): pl.pallas_call(finish, out_shape=(maps, maps, maps, image, image), in_spe...  2.13 us

profile of v4, /device:TPU:1, one launch (start us, length us, event | category | flops | bytes accessed | tf_op | source)
XLA Modules:
  0.0 46.5 jit_solution(239728930066577522)
XLA Ops:
  0.6 43.7 %shard_map.146 = (f32[8,64,128]{2,1,0:T(8,128)}, f32[64,128]{1,0:T(8,128)}, f32[64,128]{1,0:T(8,128)}, f32[8,128]{1,0:T(8,128)}) custom-call(f32[8,64,128]{2,1,0:T(8,128)} %basis_h.3, f32[64,128]{1,0:T(8,128)} %resid_a_h.1, f32[64,128]{1,0:T(8,128)} %resid_b_h.1, f32[3]{0:T(128)} %scal_h.1, f32[8,512]{1,0:T(8,128)} %pa_h.1, f32[8,512]{1,0:T(8,128)} %pb_h.1, ...), custom_call_target="tpu_custom_call" | custom-call | tf_op jit(solution)/shard_map/pallas_call | solution.py:404
  44.4 2.1 %shard_map.147 = (f32[8,64,128]{2,1,0:T(8,128)}, f32[8,64,128]{2,1,0:T(8,128)}, f32[8,64,128]{2,1,0:T(8,128)}, f32[64,128]{1,0:T(8,128)}, f32[64,128]{1,0:T(8,128)}) custom-call(f32[8,64,128]{2,1,0:T(8,128)} %get-tuple-element.9.grad_h, f32[64,128]{1,0:T(8,128)} %get-tuple-element.10.raw_a_h, f32[64,128]{1,0:T(8,128)} %get-tuple-element.11.raw_b_h, ...), custom_call_target="tpu_custom_call" | custom-call | tf_op jit(solution)/shard_map/pallas_call | solution.py:458

commit v5 on v4

--- a/solution.py
+++ b/solution.py
@@ -291,14 +291,6 @@
     gb = gb[:, :W] + gb[:, W:]
     for k in range(K):
         raw_v[k] = raw_v[k] + gb[k * R : (k + 1) * R]
-    for s, _, _ in s_d2:
-        s.wait_recv()
-    for d in (1, 2, 3):
-        put_a(d, ext_c[d])
-    ga = dot(wext_a[:, middle], ta_hi[:, middle], 1, 1) + dot(wext_a[:, middle], ta_lo[:, middle], 1, 1)
-    ga = ga[:R] + ga[R:]
-    for k in range(K):
-        raw_v[k] = raw_v[k] + ga[:, k * W : (k + 1) * W]
     s_a3.wait_recv()
     for d in range(4):
         hi, lo = split(ext_o[d])
@@ -306,10 +298,18 @@
         wext_o[d * R : (d + 1) * R, W : 2 * W] = lo
     gb = dot(to_hi[...], wext_o[...], 1, 0) + dot(to_lo[...], wext_o[...], 1, 0)
     gb = gb[:, :W] + gb[:, W:]
+    for k in range(K):
+        raw_v[k] = raw_v[k] + gb[k * R : (k + 1) * R]
+    for s, _, _ in s_d2:
+        s.wait_recv()
+    for d in (1, 2, 3):
+        put_a(d, ext_c[d])
+    ga = dot(wext_a[:, middle], ta_hi[:, middle], 1, 1) + dot(wext_a[:, middle], ta_lo[:, middle], 1, 1)
+    ga = ga[:R] + ga[R:]
     zz = jnp.zeros((R, W), f32)
     zv = jnp.zeros((R, W), f32)
     for k in range(K):
-        g = m * (raw_v[k] + gb[k * R : (k + 1) * R])
+        g = m * (raw_v[k] + ga[:, k * W : (k + 1) * W])
         raw_v[k] = g
         zz = zz + g * g
         zv = zv + g * basis[k]

time: 46.8 us -> 46.8 us (level)
  no operation moved by 1% of the time
where the time goes in v5:
time: 46.8 us; the launch traced here: 46.5 us
  Pallas kernels  45.9 us (98%)
  between operations  0.64 us (1%)
    pallas_call x1, Pallas kernels, body(): pl.pallas_call(kernel, out_shape=(maps, image, image, jax.ShapeDtypeStruc...  43.7 us
    pallas_call x1, Pallas kernels, body(): pl.pallas_call(finish, out_shape=(maps, maps, maps, image, image), in_spe...  2.13 us

profile of v5, /device:TPU:1, one launch (start us, length us, event | category | flops | bytes accessed | tf_op | source)
XLA Modules:
  0.0 46.5 jit_solution(554592273906459523)
XLA Ops:
  0.6 43.7 %shard_map.146 = (f32[8,64,128]{2,1,0:T(8,128)}, f32[64,128]{1,0:T(8,128)}, f32[64,128]{1,0:T(8,128)}, f32[8,128]{1,0:T(8,128)}) custom-call(f32[8,64,128]{2,1,0:T(8,128)} %basis_h.3, f32[64,128]{1,0:T(8,128)} %resid_a_h.1, f32[64,128]{1,0:T(8,128)} %resid_b_h.1, f32[3]{0:T(128)} %scal_h.1, f32[8,512]{1,0:T(8,128)} %pa_h.1, f32[8,512]{1,0:T(8,128)} %pb_h.1, ...), custom_call_target="tpu_custom_call" | custom-call | tf_op jit(solution)/shard_map/pallas_call | solution.py:404
  44.4 2.1 %shard_map.147 = (f32[8,64,128]{2,1,0:T(8,128)}, f32[8,64,128]{2,1,0:T(8,128)}, f32[8,64,128]{2,1,0:T(8,128)}, f32[64,128]{1,0:T(8,128)}, f32[64,128]{1,0:T(8,128)}) custom-call(f32[8,64,128]{2,1,0:T(8,128)} %get-tuple-element.9.grad_h, f32[64,128]{1,0:T(8,128)} %get-tuple-element.10.raw_a_h, f32[64,128]{1,0:T(8,128)} %get-tuple-element.11.raw_b_h, ...), custom_call_target="tpu_custom_call" | custom-call | tf_op jit(solution)/shard_map/pallas_call | solution.py:458

commit v6 on v5

--- a/solution.py
+++ b/solution.py
@@ -300,12 +300,11 @@
     gb = gb[:, :W] + gb[:, W:]
     for k in range(K):
         raw_v[k] = raw_v[k] + gb[k * R : (k + 1) * R]
-    for s, _, _ in s_d2:
+    for d, (s, _, _) in enumerate(s_d2, 1):
         s.wait_recv()
-    for d in (1, 2, 3):
-        put_a(d, ext_c[d])
-    ga = dot(wext_a[:, middle], ta_hi[:, middle], 1, 1) + dot(wext_a[:, middle], ta_lo[:, middle], 1, 1)
-    ga = ga[:R] + ga[R:]
+        put_a(4 - d, ext_c[4 - d])
+    ga = dot(wext_a[:, middle], ta_hi[:, middle], 1, 1)
+    ga = ga[:R] + ga[R:] + dot(wext_a[0:R, middle], ta_lo[:, middle], 1, 1)
     zz = jnp.zeros((R, W), f32)
     zv = jnp.zeros((R, W), f32)
     for k in range(K):

time: 46.8 us -> 46.8 us (level)
  no operation moved by 1% of the time
where the time goes in v6:
time: 46.8 us; the launch traced here: 46.5 us
  Pallas kernels  45.9 us (98%)
  between operations  0.64 us (1%)
    pallas_call x1, Pallas kernels, body(): pl.pallas_call(kernel, out_shape=(maps, image, image, jax.ShapeDtypeStruc...  43.8 us
    pallas_call x1, Pallas kernels, body(): pl.pallas_call(finish, out_shape=(maps, maps, maps, image, image), in_spe...  2.13 us

profile of v6, /device:TPU:1, one launch (start us, length us, event | category | flops | bytes accessed | tf_op | source)
XLA Modules:
  0.0 46.5 jit_solution(6791406168412617289)
XLA Ops:
  0.6 43.8 %shard_map.146 = (f32[8,64,128]{2,1,0:T(8,128)}, f32[64,128]{1,0:T(8,128)}, f32[64,128]{1,0:T(8,128)}, f32[8,128]{1,0:T(8,128)}) custom-call(f32[8,64,128]{2,1,0:T(8,128)} %basis_h.3, f32[64,128]{1,0:T(8,128)} %resid_a_h.1, f32[64,128]{1,0:T(8,128)} %resid_b_h.1, f32[3]{0:T(128)} %scal_h.1, f32[8,512]{1,0:T(8,128)} %pa_h.1, f32[8,512]{1,0:T(8,128)} %pb_h.1, ...), custom_call_target="tpu_custom_call" | custom-call | tf_op jit(solution)/shard_map/pallas_call | solution.py:403
  44.4 2.1 %shard_map.147 = (f32[8,64,128]{2,1,0:T(8,128)}, f32[8,64,128]{2,1,0:T(8,128)}, f32[8,64,128]{2,1,0:T(8,128)}, f32[64,128]{1,0:T(8,128)}, f32[64,128]{1,0:T(8,128)}) custom-call(f32[8,64,128]{2,1,0:T(8,128)} %get-tuple-element.9.grad_h, f32[64,128]{1,0:T(8,128)} %get-tuple-element.10.raw_a_h, f32[64,128]{1,0:T(8,128)} %get-tuple-element.11.raw_b_h, ...), custom_call_target="tpu_custom_call" | custom-call | tf_op jit(solution)/shard_map/pallas_call | solution.py:457
